TPU v7x, 32 devices: a whole 2x2x4 slice. The times are simulated.
32 devices in a mesh: rows: 2 (over x), specs: 16 (over z, y, core).
Axes of the slice: x: 2, y: 2, z: 4, core: 2. Of those that a mesh axis runs over, the one named last changes fastest.
Arguments:
- center: float32 [16, 512, 64], P('rows'), may hold values from -6 to 6
- radius: float32 [16, 512, 64], P('rows'), may hold values from 0.01 to 0.2
- conv_weight: float32 [3, 3, 64, 64], replicated, may hold values from -0.25 to 0.25
- conv_bias: float32 [64], replicated, may hold values from -3 to 3
- split_status: int32 [16, 512, 64], P('rows'), may hold values from 0 to 2
- out_coeffs: bfloat16 [128, 16, 512, 64], P('specs', 'rows'), may hold values from -6 to 6
- spec_ids: int32 [128], P('specs'), may hold values from 0 to 4095
- spec_offsets: float32 [4096], replicated, may hold values from -5 to 5
Outputs:
- input_coeffs: bfloat16 [128, 16, 512, 64], P('specs', 'rows')
- bounds: float32 [128], P('specs')
All inputs are finite; a program needn't handle non-finite values.
Results may differ from a plain program's by a relative error of at most 0.0052.
Values may be sent and summed in bfloat16 or wider, within the bound.
A program may use at most 128 MiB of HBM per device.

v0:
```python
import functools

import jax
import jax.numpy as jnp
from jax import lax
from jax.experimental import pallas as pl
from jax.experimental.pallas import tpu as pltpu
from jax.sharding import PartitionSpec as P

F32 = jnp.float32
BF16 = jnp.bfloat16
MESH = pl.DeviceIdType.MESH


def split2(value):
    high = value.astype(BF16)
    return high, (value - high.astype(F32)).astype(BF16)


def combine(first, middle, last):
    width = first.shape[1]
    rolled = pltpu.roll(first, 1, 1)
    lane = lax.broadcasted_iota(jnp.int32, (first.shape[0], 128), 1)
    rolled = jnp.concatenate(
        [jnp.where(lane == 0, 0.0, rolled[:, :128]), rolled[:, 128:]], axis=1
    )
    back = pltpu.roll(last, width - 1, 1)
    back = jnp.concatenate(
        [back[:, :-128], jnp.where(lane == 127, 0.0, back[:, -128:])], axis=1
    )
    return rolled + middle + back


def fold(value):
    rows, width = value.shape
    return jnp.sum(value.reshape(rows // 8, 8, width), axis=0)


def kernel(
    n_rows,
    center_hbm, radius_hbm, weight_hbm, bias_hbm, status_hbm, coeff_hbm, ids_hbm, table_hbm,
    out_ref, bounds_ref,
    center, radius, status, coeff, weight_ref, bias_ref, ids_ref, table_ref,
    low_end, high_end, slopes, icept, edge_slopes,
    box_edge, halo_box, halo_coeff, shifted, box_weight, rad_weight, back_weight, edge_weight, bias_col,
    acc, parts, table_vec,
    load_sem, coeff_sem, box_send, box_recv, pass_send, pass_recv,
    slope_send, slope_recv, spass_send, spass_recv, row_send, row_recv, part_send, part_recv,
):
    specs, rows, chans, cols = coeff.shape
    half = chans // 2
    me = lax.axis_index("rows")
    lane_dev = lax.axis_index("specs")
    core = lax.rem(lane_dev, 2)
    partner = lane_dev + 1 - 2 * core
    has_prev = me > 0
    has_next = me < n_rows - 1
    mine = pl.ds(pl.multiple_of(core * half, half), half)
    exists = (has_prev, has_next)
    sends = (has_next, has_prev)
    target = (me + 1, me - 1)
    edge = (rows - 1, 0)

    loads = [
        pltpu.make_async_copy(center_hbm, center.at[pl.ds(1, rows)], load_sem.at[0]),
        pltpu.make_async_copy(radius_hbm, radius.at[pl.ds(1, rows)], load_sem.at[1]),
        pltpu.make_async_copy(status_hbm, status, load_sem.at[2]),
    ]
    small = [
        pltpu.make_async_copy(weight_hbm, weight_ref, load_sem.at[3]),
        pltpu.make_async_copy(bias_hbm, bias_ref, load_sem.at[4]),
        pltpu.make_async_copy(ids_hbm, ids_ref, load_sem.at[5]),
        pltpu.make_async_copy(table_hbm, table_ref, load_sem.at[6]),
    ]
    for copy in loads[:2] + small + loads[2:]:
        copy.start()

    barrier = pltpu.get_barrier_semaphore()
    for step in range(1, n_rows):
        pl.semaphore_signal(
            barrier, inc=1, device_id={"rows": lax.rem(me + step, n_rows)}, device_id_type=MESH
        )
    pl.semaphore_signal(barrier, inc=1, device_id={"specs": partner}, device_id_type=MESH)

    for copy in loads[:2]:
        copy.wait()
    for d in range(2):
        for a, ref in enumerate((center, radius)):
            box_edge[d, a] = ref[1 + edge[d]].astype(BF16)
    pl.semaphore_wait(barrier, n_rows)

    def box_copy(d):
        return pltpu.make_async_remote_copy(
            src_ref=box_edge.at[d, :, mine],
            dst_ref=halo_box.at[d, :, mine],
            send_sem=box_send.at[d],
            recv_sem=box_recv.at[d],
            device_id={"rows": target[d]},
            device_id_type=MESH,
        )

    def pass_copy(d):
        return pltpu.make_async_remote_copy(
            src_ref=halo_box.at[d, :, mine],
            dst_ref=halo_box.at[d, :, mine],
            send_sem=pass_send.at[d],
            recv_sem=pass_recv.at[d],
            device_id={"specs": partner},
            device_id_type=MESH,
        )

    def slope_copy(d):
        return pltpu.make_async_remote_copy(
            src_ref=slopes.at[edge[d], mine],
            dst_ref=edge_slopes.at[d, mine],
            send_sem=slope_send.at[d],
            recv_sem=slope_recv.at[d],
            device_id={"rows": target[d]},
            device_id_type=MESH,
        )

    def spass_copy(d):
        return pltpu.make_async_remote_copy(
            src_ref=edge_slopes.at[d, mine],
            dst_ref=edge_slopes.at[d, mine],
            send_sem=spass_send.at[d],
            recv_sem=spass_recv.at[d],
            device_id={"specs": partner},
            device_id_type=MESH,
        )

    def row_copy(d, s):
        return pltpu.make_async_remote_copy(
            src_ref=coeff_hbm.at[s, edge[d]],
            dst_ref=halo_coeff.at[d, s],
            send_sem=row_send.at[d, s],
            recv_sem=row_recv.at[d, s],
            device_id={"rows": target[d]},
            device_id_type=MESH,
        )

    first = specs // 2
    for d in range(2):
        @pl.when(sends[d])
        def _():
            box_copy(d).start()

    coeff_loads = [
        pltpu.make_async_copy(coeff_hbm.at[s], coeff.at[s], coeff_sem.at[s]) for s in range(specs)
    ]
    for copy in coeff_loads:
        copy.start()

    for d in range(2):
        @pl.when(jnp.logical_not(exists[d]))
        def _():
            halo_box[d] = jnp.zeros(halo_box.shape[1:], BF16)

    for copy in small:
        copy.wait()

    zeros = jnp.zeros((chans, chans), F32)
    back = jnp.concatenate([weight_ref[2 - k, j] for k in range(3) for j in range(3)], axis=1)
    blank3 = jnp.zeros((chans, 3 * chans), F32)
    upper_rows = jnp.concatenate([back, blank3], axis=1).astype(BF16)
    lower_rows = jnp.concatenate([blank3, back], axis=1).astype(BF16)
    bias_row = bias_ref[...]
    bias_high = bias_row.astype(BF16).astype(F32)
    bias_mid = (bias_row - bias_high).astype(BF16).astype(F32)
    bias_low = bias_row - bias_high - bias_mid
    zrow = jnp.zeros((1, chans), F32)
    bias_parts = (bias_high, bias_mid, bias_low)

    def bias_rows(own):
        lines = [
            jnp.concatenate(
                [part if k in own and j == 1 else zrow for k in range(4) for j in range(3)], axis=1
            )
            for part in bias_parts
        ]
        return jnp.concatenate(lines + [jnp.zeros((13, 12 * chans), F32)], axis=0).astype(BF16)

    back_weight[...] = jnp.concatenate([upper_rows, lower_rows, bias_rows((1, 2))], axis=0)
    edge_weight[0] = jnp.concatenate([upper_rows, bias_rows((1,))], axis=0)
    edge_weight[1] = jnp.concatenate([lower_rows, bias_rows((2,))], axis=0)

    wide = jnp.concatenate(
        [
            jnp.concatenate([weight_ref[k, j] for j in range(3)] + [zeros], axis=1)
            for k in range(3)
        ]
        + [jnp.zeros((chans, 4 * chans), F32)],
        axis=0,
    )
    fore = wide.T[: 3 * chans]
    fore = jnp.concatenate([fore, pltpu.roll(fore, chans, 1)], axis=0)
    for ref, value in ((box_weight, fore), (rad_weight, jnp.abs(fore))):
        high, low = split2(value)
        ref[...] = jnp.concatenate([high, low, high], axis=1)

    for d in range(2):
        @pl.when(sends[d])
        def _():
            for s in range(first):
                row_copy(d, s).start()

    eye = lax.broadcasted_iota(jnp.int32, (chans, chans), 0) == lax.broadcasted_iota(
        jnp.int32, (chans, chans), 1
    )
    bias_col[...] = jnp.broadcast_to(
        jnp.sum(jnp.where(eye, jnp.broadcast_to(bias_row, (chans, chans)), 0.0), axis=1, keepdims=True),
        (chans, 128),
    )

    where_in_table = (
        lax.broadcasted_iota(jnp.int32, table_ref.shape, 0) * 128
        + lax.broadcasted_iota(jnp.int32, table_ref.shape, 1)
    )
    for s in range(specs):
        table_vec[pl.ds(s, 1), :] = jnp.sum(
            jnp.where(where_in_table == ids_ref[s], table_ref[...], 0.0), axis=0, keepdims=True
        )

    def field(four_rows, weight):
        high, low = split2(four_rows)
        return jnp.dot(
            weight, jnp.concatenate([high, high, low], axis=0), preferred_element_type=F32
        )

    def relax(h, c_res, r_res):
        blocks = [slice(j * chans, (j + 1) * chans) for j in range(3)]
        center_out = combine(*(c_res[b] for b in blocks)) + bias_col[:, :1]
        radius_out = combine(*(r_res[b] for b in blocks))
        upper = center_out + radius_out
        lower = center_out - radius_out
        spread = 2.0 * radius_out
        relaxed = jnp.minimum(jnp.maximum(upper, 0.0), spread) / spread
        state = status[h]
        slope = jnp.where(state == 2, relaxed, jnp.where(state == 1, 1.0, 0.0))
        slopes[h] = slope.astype(BF16)
        cut = jnp.where(state == 2, -relaxed * jnp.minimum(lower, 0.0), 0.0)
        icept[h] = cut.astype(BF16).astype(F32)
        low_end[h] = center[h + 1] - radius[h + 1]
        high_end[h] = center[h + 1] + radius[h + 1]

    loads[2].wait()
    pairs = (rows - 2) // 2

    def inner_slopes(p):
        h = 1 + 2 * p
        four = lambda ref: ref[pl.ds(h, 4)].reshape(4 * chans, cols)
        c_res = field(four(center), box_weight[...])
        r_res = field(four(radius), rad_weight[...])
        for r in range(2):
            block = slice(3 * chans * r, 3 * chans * (r + 1))
            relax(h + r, c_res[block], r_res[block])

    inner_slopes(0)
    for d in range(2):
        @pl.when(exists[d])
        def _():
            box_copy(d).wait_recv()
            pass_copy(d).start()
    inner_slopes(1)
    for d in range(2):
        @pl.when(exists[d])
        def _():
            pass_copy(d).wait()

    blank = jnp.zeros((chans, cols), F32)
    for d, ref_row in ((0, 0), (1, rows - 1)):
        def three(a, ref):
            own = [ref[1], ref[2]] if d == 0 else [ref[rows - 1], ref[rows]]
            halo = [halo_box[d, a].astype(F32)]
            return jnp.concatenate((halo + own if d == 0 else own + halo) + [blank], axis=0)

        c_res = field(three(0, center), box_weight[pl.ds(0, 3 * chans)])
        r_res = field(three(1, radius), rad_weight[pl.ds(0, 3 * chans)])
        relax(ref_row, c_res, r_res)

    for d in range(2):
        @pl.when(sends[d])
        def _():
            slope_copy(d).start()
            for s in range(first, specs):
                row_copy(d, s).start()
    for p in range(2, pairs):
        inner_slopes(p)

    def finish(s, h, value):
        out_ref[s, h] = value.astype(BF16)
        return fold(jnp.minimum(value * low_end[h], value * high_end[h]))

    lane = lax.broadcasted_iota(jnp.int32, (chans, 128), 1)

    def shifts(pre):
        none = jnp.zeros((chans, 128), BF16)
        ahead = pltpu.roll(pre, cols - 1, 1)
        ahead = jnp.concatenate(
            [ahead[:, :-128], jnp.where(lane == 127, none, ahead[:, -128:])], axis=1
        )
        behind = pltpu.roll(pre, 1, 1)
        behind = jnp.concatenate(
            [jnp.where(lane == 0, none, behind[:, :128]), behind[:, 128:]], axis=1
        )
        return ahead, pre, behind

    def edge_row(s, d, halo):
        h = 0 if d == 0 else rows - 1
        own = pl.ds(0, 3) if d == 0 else pl.ds(rows - 3, 3)
        near = shifted[s, own].reshape(9 * chans, cols)
        four = jnp.concatenate([*halo, near] if d == 0 else [near, *halo], axis=0)
        result = jnp.dot(edge_weight[d], four, preferred_element_type=F32)
        acc[s] += finish(s, h, result[:chans]) + fold(result[chans:])

    for copy in coeff_loads:
        copy.wait()

    def inner(s, carry):
        total = jnp.zeros((8, cols), F32)
        for h in range(rows):
            block = coeff[s, h]
            for j, moved in enumerate(shifts(block * slopes[h])):
                shifted[s, h, j] = moved
            total += fold(jnp.minimum(block, 0).astype(F32) * icept[h])
        for p in range(pairs):
            h = 1 + 2 * p
            pre = shifted[s, pl.ds(h - 1, 4)].reshape(12 * chans, cols)
            result = jnp.dot(back_weight[...], pre, preferred_element_type=F32)
            for r in range(2):
                total += finish(s, h + r, result[chans * r : chans * (r + 1)])
            total += fold(result[2 * chans :])
        acc[s] = total
        return carry

    lax.fori_loop(0, specs // 2, inner, 0)
    for d in range(2):
        @pl.when(exists[d])
        def _():
            slope_copy(d).wait_recv()
            spass_copy(d).start()
    lax.fori_loop(specs // 2, specs, inner, 0)

    for d in range(2):
        @pl.when(jnp.logical_not(exists[d]))
        def _():
            def at_border(s, carry):
                edge_row(s, d, [jnp.zeros((3 * chans, cols), BF16)])
                return carry

            lax.fori_loop(0, specs, at_border, 0)

    for d in range(2):
        @pl.when(exists[d])
        def _():
            spass_copy(d).wait()

            def at_halo(s, carry):
                row_copy(d, s).wait_recv()
                edge_row(s, d, shifts(halo_coeff[d, s] * edge_slopes[d]))
                return carry

            lax.fori_loop(0, specs, at_halo, 0)

    folded = jnp.sum(acc[...], axis=1)
    share = folded[:, :128]
    for t in range(1, cols // 128):
        share += folded[:, 128 * t : 128 * (t + 1)]
    parts[0] = share

    def part_copy(step):
        return pltpu.make_async_remote_copy(
            src_ref=parts.at[0],
            dst_ref=parts.at[step],
            send_sem=part_send.at[step],
            recv_sem=part_recv.at[step],
            device_id={"rows": lax.rem(me + step, n_rows)},
            device_id_type=MESH,
        )

    for step in range(1, n_rows):
        part_copy(step).start()
    for d in range(2):
        @pl.when(sends[d])
        def _():
            box_copy(d).wait_send()
            slope_copy(d).wait_send()
            for s in range(specs):
                row_copy(d, s).wait_send()
    for step in range(1, n_rows):
        part_copy(step).wait()
    total = parts[0]
    for step in range(1, n_rows):
        total += parts[step]
    bound = jnp.sum(
        total * (1.0 / (rows * n_rows * cols)) + table_vec[...], axis=1, keepdims=True
    )
    shape = (specs, 128)
    diagonal = lax.broadcasted_iota(jnp.int32, shape, 0) == lax.broadcasted_iota(
        jnp.int32, shape, 1
    )
    line = jnp.sum(jnp.where(diagonal, jnp.broadcast_to(bound, shape), 0.0), axis=0, keepdims=True)
    bounds_ref[...] = line[:, :specs]


def store_kernel(out_vmem, bounds_vmem, out_hbm, bounds_hbm, sem):
    specs = out_vmem.shape[0]
    copies = [
        pltpu.make_async_copy(out_vmem.at[s], out_hbm.at[s], sem.at[s]) for s in range(specs)
    ]
    copies.append(pltpu.make_async_copy(bounds_vmem, bounds_hbm, sem.at[specs]))
    for copy in copies:
        copy.start()
    for copy in copies:
        copy.wait()


def per_device(
    center, radius, conv_weight, conv_bias, split_status, out_coeffs, spec_ids, spec_offsets
):
    n_rows = lax.axis_size("rows")
    specs, rows, cols, chans = out_coeffs.shape
    swap3 = lambda x: jnp.transpose(x, (0, 2, 1))
    dma = pltpu.SemaphoreType.DMA
    vmem = pl.BlockSpec(memory_space=pltpu.VMEM)
    out, bounds = pl.pallas_call(
        functools.partial(kernel, n_rows),
        out_shape=(
            pltpu.VMEM((specs, rows, chans, cols), BF16),
            pltpu.VMEM((1, specs), F32),
        ),
        in_specs=[
            pl.BlockSpec(memory_space=pltpu.HBM),
        ] * 8,
        out_specs=(vmem, vmem),
        scratch_shapes=[
            pltpu.VMEM((rows + 2, chans, cols), F32),
            pltpu.VMEM((rows + 2, chans, cols), F32),
            pltpu.VMEM((rows, chans, cols), jnp.int32),
            pltpu.VMEM((specs, rows, chans, cols), BF16),
            pltpu.VMEM(conv_weight.shape, F32),
            pltpu.VMEM((1, chans), F32),
            pltpu.SMEM((specs,), jnp.int32),
            pltpu.VMEM((spec_offsets.shape[0] // 128, 128), F32),
            pltpu.VMEM((rows, chans, cols), F32),
            pltpu.VMEM((rows, chans, cols), F32),
            pltpu.VMEM((rows, chans, cols), BF16),
            pltpu.VMEM((rows, chans, cols), F32),
            pltpu.VMEM((2, chans, cols), BF16),
            pltpu.VMEM((2, 2, chans, cols), BF16),
            pltpu.VMEM((2, 2, chans, cols), BF16),
            pltpu.VMEM((2, specs, chans, cols), BF16),
            pltpu.VMEM((specs, rows, 3, chans, cols), BF16),
            pltpu.VMEM((6 * chans, 12 * chans), BF16),
            pltpu.VMEM((6 * chans, 12 * chans), BF16),
            pltpu.VMEM((2 * chans + 16, 12 * chans), BF16),
            pltpu.VMEM((2, chans + 16, 12 * chans), BF16),
            pltpu.VMEM((chans, 128), F32),
            pltpu.VMEM((specs, 8, cols), F32),
            pltpu.VMEM((n_rows, specs, 128), F32),
            pltpu.VMEM((specs, 128), F32),
            dma((7,)), dma((specs,)),
            dma((2,)), dma((2,)), dma((2,)), dma((2,)),
            dma((2,)), dma((2,)), dma((2,)), dma((2,)),
            dma((2, specs)), dma((2, specs)), dma((n_rows,)), dma((n_rows,)),
        ],
        compiler_params=pltpu.CompilerParams(
            collective_id=0, has_side_effects=True, vmem_limit_bytes=48 * 1024 * 1024
        ),
        name="bound_pass",
    )(
        *(
            pltpu.with_memory_space_constraint(x, pltpu.HBM)
            for x in (
                swap3(center),
                swap3(radius),
                conv_weight,
                conv_bias.reshape(1, chans),
                swap3(split_status),
                jnp.transpose(out_coeffs, (0, 1, 3, 2)),
                spec_ids,
                spec_offsets.reshape(-1, 128),
            )
        )
    )
    hbm = pl.BlockSpec(memory_space=pltpu.HBM)
    out, bounds = pl.pallas_call(
        store_kernel,
        out_shape=(
            jax.ShapeDtypeStruct((specs, rows, chans, cols), BF16),
            jax.ShapeDtypeStruct((1, specs), F32),
        ),
        in_specs=[vmem, vmem],
        out_specs=(hbm, hbm),
        scratch_shapes=[dma((specs + 1,))],
        compiler_params=pltpu.CompilerParams(vmem_limit_bytes=1024 * 1024),
        name="store",
    )(*(pltpu.with_memory_space_constraint(x, pltpu.VMEM) for x in (out, bounds)))
    return jnp.transpose(out, (0, 1, 3, 2)), bounds.reshape(specs)


def solution(mesh):
    in_specs = (
        P("rows", None, None),
        P("rows", None, None),
        P(),
        P(),
        P("rows", None, None),
        P("specs", "rows", None, None),
        P("specs"),
        P(),
    )
    out_specs = (P("specs", "rows", None, None), P("specs"))
    return jax.shard_map(
        per_device, mesh=mesh, in_specs=in_specs, out_specs=out_specs, check_vma=False
    )
```

profile of v0, /device:TPU:0, one launch (start us, length us, event | category | flops | bytes accessed | tf_op | source)
XLA Modules:
  0.0 26.1 jit_solution(4639717589456202572)
XLA Ops:
  0.6 23.4 %bound_pass.1 = (bf16[8,8,64,512]{3,2,1,0:T(8,128)(2,1)S(1)}, f32[1,8]{1,0:T(1,128)S(1)}) custom-call(f32[8,64,512]{2,1,0:T(8,128)} %bitcast.9, f32[8,64,512]{2,1,0:T(8,128)} %bitcast.10, f32[3,3,64,64]{3,2,1,0:T(8,128)} %weight_hbm.1, f32[1,64]{1,0:T(1,128)} %bitcast.13, s32[8,64,512]{2,1,0:T(8,128)} %bitcast.11, bf16[8,8,64,512]{3,2,1,0:T(8,128)(2,1)} %bitcast.8, ...), custom_call_target="tpu_custom_call" | custom-call | tf_op jit(solution)/shard_map/bound_pass/pallas_call | solution.py:426
  24.0 2.1 %store.1 = (bf16[8,8,64,512]{3,2,1,0:T(8,128)(2,1)}, f32[1,8]{1,0:T(1,128)}) custom-call(bf16[8,8,64,512]{3,2,1,0:T(8,128)(2,1)S(1)} %get-tuple-element.6.out_vmem, f32[1,8]{1,0:T(1,128)S(1)} %get-tuple-element.7.bounds_vmem), custom_call_target="tpu_custom_call" | custom-call | tf_op jit(solution)/shard_map/store/pallas_call | solution.py:487
where the time goes:
time: 26.2 us; the launch traced here: 26.1 us
  Pallas kernels  25.5 us (97%)
  between operations  0.64 us (2%)
    pallas_call x1, Pallas kernels, per_device(): pl.pallas_call(functools.partial(kernel, n_rows), out_shape=(pltpu.VMEM((...  23.4 us
    pallas_call x1, Pallas kernels, per_device(): pl.pallas_call(store_kernel, out_shape=(jax.ShapeDtypeStruct((specs, rows...  2.08 us

commit v1 on v0

--- a/solution.py
+++ b/solution.py
@@ -144,6 +144,8 @@
         @pl.when(sends[d])
         def _():
             box_copy(d).start()
+            for s in range(first):
+                row_copy(d, s).start()
 
     coeff_loads = [
         pltpu.make_async_copy(coeff_hbm.at[s], coeff.at[s], coeff_sem.at[s]) for s in range(specs)
@@ -194,15 +196,9 @@
     )
     fore = wide.T[: 3 * chans]
     fore = jnp.concatenate([fore, pltpu.roll(fore, chans, 1)], axis=0)
-    for ref, value in ((box_weight, fore), (rad_weight, jnp.abs(fore))):
-        high, low = split2(value)
-        ref[...] = jnp.concatenate([high, low, high], axis=1)
-
-    for d in range(2):
-        @pl.when(sends[d])
-        def _():
-            for s in range(first):
-                row_copy(d, s).start()
+    high, low = split2(fore)
+    box_weight[...] = jnp.concatenate([high, low, high], axis=1)
+    rad_weight[...] = jnp.abs(fore).astype(BF16)
 
     eye = lax.broadcasted_iota(jnp.int32, (chans, chans), 0) == lax.broadcasted_iota(
         jnp.int32, (chans, chans), 1
@@ -226,6 +222,9 @@
         return jnp.dot(
             weight, jnp.concatenate([high, high, low], axis=0), preferred_element_type=F32
         )
+
+    def plain(four_rows, weight):
+        return jnp.dot(weight, four_rows.astype(BF16), preferred_element_type=F32)
 
     def relax(h, c_res, r_res):
         blocks = [slice(j * chans, (j + 1) * chans) for j in range(3)]
@@ -250,7 +249,7 @@
         h = 1 + 2 * p
         four = lambda ref: ref[pl.ds(h, 4)].reshape(4 * chans, cols)
         c_res = field(four(center), box_weight[...])
-        r_res = field(four(radius), rad_weight[...])
+        r_res = plain(four(radius), rad_weight[...])
         for r in range(2):
             block = slice(3 * chans * r, 3 * chans * (r + 1))
             relax(h + r, c_res[block], r_res[block])
@@ -275,7 +274,7 @@
             return jnp.concatenate((halo + own if d == 0 else own + halo) + [blank], axis=0)
 
         c_res = field(three(0, center), box_weight[pl.ds(0, 3 * chans)])
-        r_res = field(three(1, radius), rad_weight[pl.ds(0, 3 * chans)])
+        r_res = plain(three(1, radius), rad_weight[pl.ds(0, 3 * chans)])
         relax(ref_row, c_res, r_res)
 
     for d in range(2):
@@ -452,7 +451,7 @@
             pltpu.VMEM((2, specs, chans, cols), BF16),
             pltpu.VMEM((specs, rows, 3, chans, cols), BF16),
             pltpu.VMEM((6 * chans, 12 * chans), BF16),
-            pltpu.VMEM((6 * chans, 12 * chans), BF16),
+            pltpu.VMEM((6 * chans, 4 * chans), BF16),
             pltpu.VMEM((2 * chans + 16, 12 * chans), BF16),
             pltpu.VMEM((2, chans + 16, 12 * chans), BF16),
             pltpu.VMEM((chans, 128), F32),

time: 26.2 us -> 25.9 us (0.989)
  Pallas kernels: 25.5 us -> 25.2 us
    pallas_call x1, Pallas kernels: 23.4 us -> 23.1 us  [per_device(): pl.pallas_call(functools.partial(kernel, n_rows), out_shape=(pltpu.VMEM((...]
where the time goes in v1:
time: 25.9 us; the launch traced here: 25.8 us
  Pallas kernels  25.2 us (97%)
  between operations  0.64 us (2%)
    pallas_call x1, Pallas kernels, per_device(): pl.pallas_call(functools.partial(kernel, n_rows), out_shape=(pltpu.VMEM((...  23.1 us
    pallas_call x1, Pallas kernels, per_device(): pl.pallas_call(store_kernel, out_shape=(jax.ShapeDtypeStruct((specs, rows...  2.08 us

profile of v1, /device:TPU:0, one launch (start us, length us, event | category | flops | bytes accessed | tf_op | source)
XLA Modules:
  0.0 25.8 jit_solution(10476890120097697280)
XLA Ops:
  0.6 23.1 %bound_pass.1 = (bf16[8,8,64,512]{3,2,1,0:T(8,128)(2,1)S(1)}, f32[1,8]{1,0:T(1,128)S(1)}) custom-call(f32[8,64,512]{2,1,0:T(8,128)} %bitcast.9, f32[8,64,512]{2,1,0:T(8,128)} %bitcast.10, f32[3,3,64,64]{3,2,1,0:T(8,128)} %weight_hbm.1, f32[1,64]{1,0:T(1,128)} %bitcast.13, s32[8,64,512]{2,1,0:T(8,128)} %bitcast.11, bf16[8,8,64,512]{3,2,1,0:T(8,128)(2,1)} %bitcast.8, ...), custom_call_target="tpu_custom_call" | custom-call | tf_op jit(solution)/shard_map/bound_pass/pallas_call | solution.py:425
  23.7 2.1 %store.1 = (bf16[8,8,64,512]{3,2,1,0:T(8,128)(2,1)}, f32[1,8]{1,0:T(1,128)}) custom-call(bf16[8,8,64,512]{3,2,1,0:T(8,128)(2,1)S(1)} %get-tuple-element.6.out_vmem, f32[1,8]{1,0:T(1,128)S(1)} %get-tuple-element.7.bounds_vmem), custom_call_target="tpu_custom_call" | custom-call | tf_op jit(solution)/shard_map/store/pallas_call | solution.py:486

commit v2 on v1

--- a/solution.py
+++ b/solution.py
@@ -139,7 +139,7 @@
             device_id_type=MESH,
         )
 
-    first = specs // 2
+    first = specs * 5 // 8
     for d in range(2):
         @pl.when(sends[d])
         def _():
@@ -254,36 +254,7 @@
             block = slice(3 * chans * r, 3 * chans * (r + 1))
             relax(h + r, c_res[block], r_res[block])
 
-    inner_slopes(0)
-    for d in range(2):
-        @pl.when(exists[d])
-        def _():
-            box_copy(d).wait_recv()
-            pass_copy(d).start()
-    inner_slopes(1)
-    for d in range(2):
-        @pl.when(exists[d])
-        def _():
-            pass_copy(d).wait()
-
-    blank = jnp.zeros((chans, cols), F32)
-    for d, ref_row in ((0, 0), (1, rows - 1)):
-        def three(a, ref):
-            own = [ref[1], ref[2]] if d == 0 else [ref[rows - 1], ref[rows]]
-            halo = [halo_box[d, a].astype(F32)]
-            return jnp.concatenate((halo + own if d == 0 else own + halo) + [blank], axis=0)
-
-        c_res = field(three(0, center), box_weight[pl.ds(0, 3 * chans)])
-        r_res = plain(three(1, radius), rad_weight[pl.ds(0, 3 * chans)])
-        relax(ref_row, c_res, r_res)
-
-    for d in range(2):
-        @pl.when(sends[d])
-        def _():
-            slope_copy(d).start()
-            for s in range(first, specs):
-                row_copy(d, s).start()
-    for p in range(2, pairs):
+    for p in range(pairs):
         inner_slopes(p)
 
     def finish(s, h, value):
@@ -315,14 +286,13 @@
     for copy in coeff_loads:
         copy.wait()
 
-    def inner(s, carry):
-        total = jnp.zeros((8, cols), F32)
-        for h in range(rows):
+    def rows_and_pairs(s, total, own_rows, own_pairs):
+        for h in own_rows:
             block = coeff[s, h]
             for j, moved in enumerate(shifts(block * slopes[h])):
                 shifted[s, h, j] = moved
             total += fold(jnp.minimum(block, 0).astype(F32) * icept[h])
-        for p in range(pairs):
+        for p in own_pairs:
             h = 1 + 2 * p
             pre = shifted[s, pl.ds(h - 1, 4)].reshape(12 * chans, cols)
             result = jnp.dot(back_weight[...], pre, preferred_element_type=F32)
@@ -330,16 +300,52 @@
                 total += finish(s, h + r, result[chans * r : chans * (r + 1)])
             total += fold(result[2 * chans :])
         acc[s] = total
+
+    def inside(s, carry):
+        blank_total = jnp.zeros((8, cols), F32)
+        rows_and_pairs(s, blank_total, range(1, rows - 1), range(1, pairs - 1))
         return carry
 
-    lax.fori_loop(0, specs // 2, inner, 0)
+    def outside(s, carry):
+        rows_and_pairs(s, acc[s], (0, rows - 1), sorted({0, pairs - 1}))
+        return carry
+
+    for d in range(2):
+        @pl.when(exists[d])
+        def _():
+            box_copy(d).wait_recv()
+            pass_copy(d).start()
+    lax.fori_loop(0, specs // 2, inside, 0)
+    for d in range(2):
+        @pl.when(exists[d])
+        def _():
+            pass_copy(d).wait()
+
+    blank = jnp.zeros((chans, cols), F32)
+    for d, ref_row in ((0, 0), (1, rows - 1)):
+        def three(a, ref):
+            own = [ref[1], ref[2]] if d == 0 else [ref[rows - 1], ref[rows]]
+            halo = [halo_box[d, a].astype(F32)]
+            return jnp.concatenate((halo + own if d == 0 else own + halo) + [blank], axis=0)
+
+        c_res = field(three(0, center), box_weight[pl.ds(0, 3 * chans)])
+        r_res = plain(three(1, radius), rad_weight[pl.ds(0, 3 * chans)])
+        relax(ref_row, c_res, r_res)
+
+    for d in range(2):
+        @pl.when(sends[d])
+        def _():
+            slope_copy(d).start()
+            for s in range(first, specs):
+                row_copy(d, s).start()
+    lax.fori_loop(specs // 2, specs, inside, 0)
+    lax.fori_loop(0, specs // 2, outside, 0)
     for d in range(2):
         @pl.when(exists[d])
         def _():
             slope_copy(d).wait_recv()
             spass_copy(d).start()
-    lax.fori_loop(specs // 2, specs, inner, 0)
-
+    lax.fori_loop(specs // 2, specs, outside, 0)
     for d in range(2):
         @pl.when(jnp.logical_not(exists[d]))
         def _():

time: 25.9 us -> 27.5 us (1.062)
  Pallas kernels: 25.2 us -> 26.7 us
    pallas_call x1, Pallas kernels: 23.1 us -> 24.6 us  [per_device(): pl.pallas_call(functools.partial(kernel, n_rows), out_shape=(pltpu.VMEM((...]
where the time goes in v2:
time: 27.5 us; the launch traced here: 27.4 us
  Pallas kernels  26.7 us (97%)
  between operations  0.64 us (2%)
    pallas_call x1, Pallas kernels, per_device(): pl.pallas_call(functools.partial(kernel, n_rows), out_shape=(pltpu.VMEM((...  24.6 us
    pallas_call x1, Pallas kernels, per_device(): pl.pallas_call(store_kernel, out_shape=(jax.ShapeDtypeStruct((specs, rows...  2.08 us

profile of v2, /device:TPU:0, one launch (start us, length us, event | category | flops | bytes accessed | tf_op | source)
XLA Modules:
  0.0 27.4 jit_solution(11912593191662107671)
XLA Ops:
  0.6 24.6 %bound_pass.1 = (bf16[8,8,64,512]{3,2,1,0:T(8,128)(2,1)S(1)}, f32[1,8]{1,0:T(1,128)S(1)}) custom-call(f32[8,64,512]{2,1,0:T(8,128)} %bitcast.9, f32[8,64,512]{2,1,0:T(8,128)} %bitcast.10, f32[3,3,64,64]{3,2,1,0:T(8,128)} %weight_hbm.1, f32[1,64]{1,0:T(1,128)} %bitcast.13, s32[8,64,512]{2,1,0:T(8,128)} %bitcast.11, bf16[8,8,64,512]{3,2,1,0:T(8,128)(2,1)} %bitcast.8, ...), custom_call_target="tpu_custom_call" | custom-call | tf_op jit(solution)/shard_map/bound_pass/pallas_call | solution.py:431
  25.3 2.1 %store.1 = (bf16[8,8,64,512]{3,2,1,0:T(8,128)(2,1)}, f32[1,8]{1,0:T(1,128)}) custom-call(bf16[8,8,64,512]{3,2,1,0:T(8,128)(2,1)S(1)} %get-tuple-element.6.out_vmem, f32[1,8]{1,0:T(1,128)S(1)} %get-tuple-element.7.bounds_vmem), custom_call_target="tpu_custom_call" | custom-call | tf_op jit(solution)/shard_map/store/pallas_call | solution.py:492

commit v3 on v1

--- a/solution.py
+++ b/solution.py
@@ -59,7 +59,7 @@
     exists = (has_prev, has_next)
     sends = (has_next, has_prev)
     target = (me + 1, me - 1)
-    edge = (rows - 1, 0)
+    sent_row = (rows - 1, 0)
 
     loads = [
         pltpu.make_async_copy(center_hbm, center.at[pl.ds(1, rows)], load_sem.at[0]),
@@ -86,7 +86,7 @@
         copy.wait()
     for d in range(2):
         for a, ref in enumerate((center, radius)):
-            box_edge[d, a] = ref[1 + edge[d]].astype(BF16)
+            box_edge[d, a] = ref[1 + sent_row[d]].astype(BF16)
     pl.semaphore_wait(barrier, n_rows)
 
     def box_copy(d):
@@ -111,7 +111,7 @@
 
     def slope_copy(d):
         return pltpu.make_async_remote_copy(
-            src_ref=slopes.at[edge[d], mine],
+            src_ref=slopes.at[sent_row[d], mine],
             dst_ref=edge_slopes.at[d, mine],
             send_sem=slope_send.at[d],
             recv_sem=slope_recv.at[d],
@@ -131,7 +131,7 @@
 
     def row_copy(d, s):
         return pltpu.make_async_remote_copy(
-            src_ref=coeff_hbm.at[s, edge[d]],
+            src_ref=coeff_hbm.at[s, sent_row[d]],
             dst_ref=halo_coeff.at[d, s],
             send_sem=row_send.at[d, s],
             recv_sem=row_recv.at[d, s],
@@ -183,8 +183,20 @@
         return jnp.concatenate(lines + [jnp.zeros((13, 12 * chans), F32)], axis=0).astype(BF16)
 
     back_weight[...] = jnp.concatenate([upper_rows, lower_rows, bias_rows((1, 2))], axis=0)
-    edge_weight[0] = jnp.concatenate([upper_rows, bias_rows((1,))], axis=0)
-    edge_weight[1] = jnp.concatenate([lower_rows, bias_rows((2,))], axis=0)
+    edge = jnp.concatenate(
+        [
+            jnp.concatenate([weight_ref[2 - k, 2 - j] for k in range(3)] + [zeros], axis=1)
+            for j in range(3)
+        ],
+        axis=0,
+    )
+    for d, block in ((0, edge), (1, pltpu.roll(edge, chans, 1))):
+        lines = [
+            jnp.concatenate([part if k == 1 + d else zrow for k in range(4)], axis=1)
+            for part in bias_parts
+        ]
+        lines.append(jnp.zeros((13, 4 * chans), F32))
+        edge_weight[d] = jnp.concatenate([block] + lines, axis=0).astype(BF16)
 
     wide = jnp.concatenate(
         [
@@ -307,10 +319,11 @@
     def edge_row(s, d, halo):
         h = 0 if d == 0 else rows - 1
         own = pl.ds(0, 3) if d == 0 else pl.ds(rows - 3, 3)
-        near = shifted[s, own].reshape(9 * chans, cols)
-        four = jnp.concatenate([*halo, near] if d == 0 else [near, *halo], axis=0)
+        near = shifted[s, own, 1].reshape(3 * chans, cols)
+        four = jnp.concatenate([halo, near] if d == 0 else [near, halo], axis=0)
         result = jnp.dot(edge_weight[d], four, preferred_element_type=F32)
-        acc[s] += finish(s, h, result[:chans]) + fold(result[chans:])
+        value = combine(*(result[j * chans : (j + 1) * chans] for j in range(3)))
+        acc[s] += finish(s, h, value) + fold(result[3 * chans :])
 
     for copy in coeff_loads:
         copy.wait()
@@ -344,7 +357,7 @@
         @pl.when(jnp.logical_not(exists[d]))
         def _():
             def at_border(s, carry):
-                edge_row(s, d, [jnp.zeros((3 * chans, cols), BF16)])
+                edge_row(s, d, jnp.zeros((chans, cols), BF16))
                 return carry
 
             lax.fori_loop(0, specs, at_border, 0)
@@ -356,7 +369,7 @@
 
             def at_halo(s, carry):
                 row_copy(d, s).wait_recv()
-                edge_row(s, d, shifts(halo_coeff[d, s] * edge_slopes[d]))
+                edge_row(s, d, halo_coeff[d, s] * edge_slopes[d])
                 return carry
 
             lax.fori_loop(0, specs, at_halo, 0)
@@ -453,7 +466,7 @@
             pltpu.VMEM((6 * chans, 12 * chans), BF16),
             pltpu.VMEM((6 * chans, 4 * chans), BF16),
             pltpu.VMEM((2 * chans + 16, 12 * chans), BF16),
-            pltpu.VMEM((2, chans + 16, 12 * chans), BF16),
+            pltpu.VMEM((2, 3 * chans + 16, 4 * chans), BF16),
             pltpu.VMEM((chans, 128), F32),
             pltpu.VMEM((specs, 8, cols), F32),
             pltpu.VMEM((n_rows, specs, 128), F32),

time: 25.9 us -> 26.3 us (1.015)
  Pallas kernels: 25.2 us -> 25.5 us
    pallas_call x1, Pallas kernels: 23.1 us -> 23.4 us  [per_device(): pl.pallas_call(functools.partial(kernel, n_rows), out_shape=(pltpu.VMEM((...]
where the time goes in v3:
time: 26.3 us; the launch traced here: 26.1 us
  Pallas kernels  25.5 us (97%)
  between operations  0.64 us (2%)
    pallas_call x1, Pallas kernels, per_device(): pl.pallas_call(functools.partial(kernel, n_rows), out_shape=(pltpu.VMEM((...  23.4 us
    pallas_call x1, Pallas kernels, per_device(): pl.pallas_call(store_kernel, out_shape=(jax.ShapeDtypeStruct((specs, rows...  2.08 us

profile of v3, /device:TPU:0, one launch (start us, length us, event | category | flops | bytes accessed | tf_op | source)
XLA Modules:
  0.0 26.1 jit_solution(5890472014072749269)
XLA Ops:
  0.6 23.4 %bound_pass.1 = (bf16[8,8,64,512]{3,2,1,0:T(8,128)(2,1)S(1)}, f32[1,8]{1,0:T(1,128)S(1)}) custom-call(f32[8,64,512]{2,1,0:T(8,128)} %bitcast.9, f32[8,64,512]{2,1,0:T(8,128)} %bitcast.10, f32[3,3,64,64]{3,2,1,0:T(8,128)} %weight_hbm.1, f32[1,64]{1,0:T(1,128)} %bitcast.13, s32[8,64,512]{2,1,0:T(8,128)} %bitcast.11, bf16[8,8,64,512]{3,2,1,0:T(8,128)(2,1)} %bitcast.8, ...), custom_call_target="tpu_custom_call" | custom-call | tf_op jit(solution)/shard_map/bound_pass/pallas_call | solution.py:438
  24.0 2.1 %store.1 = (bf16[8,8,64,512]{3,2,1,0:T(8,128)(2,1)}, f32[1,8]{1,0:T(1,128)}) custom-call(bf16[8,8,64,512]{3,2,1,0:T(8,128)(2,1)S(1)} %get-tuple-element.6.out_vmem, f32[1,8]{1,0:T(1,128)S(1)} %get-tuple-element.7.bounds_vmem), custom_call_target="tpu_custom_call" | custom-call | tf_op jit(solution)/shard_map/store/pallas_call | solution.py:499
